TPU v7x, 256 devices: a whole 4x4x8 slice. The times are simulated.
256 devices in a mesh: ctx: 64 (over z, y, core), tsp: 4 (over x).
Axes of the slice: x: 4, y: 4, z: 8, core: 2. Of those that a mesh axis runs over, the one named last changes fastest.
Arguments:
- queries: bfloat16 [32768, 5120], P(('ctx', 'tsp')), may hold values from -6 to 6
- keys: bfloat16 [32768, 5120], P(('ctx', 'tsp')), may hold values from -6 to 6
- values: bfloat16 [32768, 5120], P(('ctx', 'tsp')), may hold values from -6 to 6
- cotangent: bfloat16 [32768, 5120], P(('ctx', 'tsp')), may hold values from -6 to 6
- content_bias: float32 [40, 128], P('tsp'), may hold values from -5 to 5
- memory_lengths: int32 [64], P('ctx'), may hold values from 0 to 1536, as said below
- segment_ends: int32 [64], P('ctx'), may hold values from 1 to 512, as said below
Outputs:
- attended: bfloat16 [32768, 5120], P(('ctx', 'tsp'))
- grad_queries: bfloat16 [32768, 5120], P(('ctx', 'tsp'))
- grad_keys: bfloat16 [32768, 5120], P(('ctx', 'tsp'))
- grad_values: bfloat16 [32768, 5120], P(('ctx', 'tsp'))
- grad_bias: float32 [40, 128], P('tsp')
Inputs may be any that keep to these rules, and one draw needn't show every extreme that they name: memory_lengths[0] is 0 and the last shard's value is 1536. `segment_ends`: a value of 512 means that the shard's first document runs to its end; shard 1 has the value 1 and the last shard the value 512.
All inputs are finite; a program needn't handle non-finite values.
Results may differ from a plain program's by a relative error of at most 0.012.
The roundings to bfloat16 on the way count: a program that leaves them out, or rounds other values in their place, can miss the bound.
Values may be sent and summed in bfloat16 or wider, within the bound.
A program may use at most 128 MiB of HBM per device.

v0:
```python
import math
import jax
import jax.numpy as jnp
from jax import lax
from jax.sharding import PartitionSpec as P

MEM = 1536


def passed_along(value, axis, steps):
    count = lax.axis_size(axis)
    initial, last = (max(0, -steps), min(count, count - steps))
    return lax.ppermute(value, axis, [(source, source + steps) for source in range(initial, last)])


def column_block(matrix, first_col, count):
    return lax.dynamic_slice_in_dim(matrix, first_col, count, 1)


def merge_heads(piece_stack):
    head_total, tok_rows, head_size = piece_stack.shape
    return jnp.transpose(piece_stack, (1, 0, 2)).reshape(tok_rows, head_total * head_size)


def shards(queries, keys, values, cotangent, content_bias, memory_lengths, segment_ends):
    q_heads, k_heads, v_heads, g_heads = (
        lax.all_to_all(queries, "tsp", split_axis=1, concat_axis=0, tiled=True),
        lax.all_to_all(keys, "tsp", split_axis=1, concat_axis=0, tiled=True),
        lax.all_to_all(values, "tsp", split_axis=1, concat_axis=0, tiled=True),
        lax.all_to_all(cotangent, "tsp", split_axis=1, concat_axis=0, tiled=True),
    )
    tok_rows = q_heads.shape[0]
    local_heads = content_bias.shape[0]
    head_size = content_bias.shape[1]
    shard_count = (MEM + tok_rows - 1) // tok_rows
    stacked = jnp.stack([k_heads, v_heads])
    blocks = []
    current = stacked
    for stride in range(shard_count):
        current = passed_along(current, "ctx", 1)
        blocks = [current] + blocks
    window = jnp.concatenate(blocks, axis=1)
    position = lax.axis_index("ctx")
    usable = jnp.minimum(memory_lengths[0], position * tok_rows)
    boundary = segment_ends[0]
    span_rows = MEM + tok_rows
    row_index = lax.broadcasted_iota(jnp.int32, (tok_rows, span_rows), 0)
    col_index = lax.broadcasted_iota(jnp.int32, (tok_rows, span_rows), 1)
    offset = col_index - MEM
    memory_ok = (col_index < MEM) & (col_index >= MEM - usable) & (row_index < boundary)
    local_ok = (
        (col_index >= MEM) & (offset <= row_index) & ((row_index < boundary) == (offset < boundary))
    )
    allowed = memory_ok | local_ok
    scaling = 1.0 / math.sqrt(head_size)
    contract_cols = (((1,), (1,)), ((), ()))
    contract_rows = (((0,), (0,)), ((), ()))

    def one_head(head_index):
        first_col = head_index * head_size
        query_rows = column_block(q_heads, first_col, head_size)
        head_bias = lax.dynamic_slice_in_dim(content_bias, head_index, 1, 0)
        shifted = (query_rows.astype(jnp.float32) + head_bias).astype(jnp.bfloat16)
        key_rows = jnp.concatenate(
            [
                column_block(window[0], first_col, head_size),
                column_block(k_heads, first_col, head_size),
            ],
            axis=0,
        )
        value_rows = jnp.concatenate(
            [
                column_block(window[1], first_col, head_size),
                column_block(v_heads, first_col, head_size),
            ],
            axis=0,
        )
        grad_rows = column_block(g_heads, first_col, head_size)
        scores = (
            lax.dot_general(shifted, key_rows, contract_cols, preferred_element_type=jnp.float32)
            * scaling
        )
        scores = jnp.where(allowed, scores, -jnp.inf)
        row_peak = jnp.max(scores, axis=1, keepdims=True)
        weights = jnp.exp(scores - row_peak)
        probs_full = weights / jnp.sum(weights, axis=1, keepdims=True)
        probs_half = probs_full.astype(jnp.bfloat16)
        attended = jnp.dot(probs_half, value_rows, preferred_element_type=jnp.float32).astype(
            jnp.bfloat16
        )
        grad_probs = lax.dot_general(
            grad_rows, value_rows, contract_cols, preferred_element_type=jnp.float32
        )
        centre = jnp.sum(probs_full * grad_probs, axis=1, keepdims=True)
        grad_scores = (probs_full * (grad_probs - centre) * scaling).astype(jnp.bfloat16)
        grad_query = jnp.dot(grad_scores, key_rows, preferred_element_type=jnp.float32)
        grad_key = lax.dot_general(
            grad_scores[:, MEM:], shifted, contract_rows, preferred_element_type=jnp.float32
        ).astype(jnp.bfloat16)
        grad_value = lax.dot_general(
            probs_half[:, MEM:], grad_rows, contract_rows, preferred_element_type=jnp.float32
        ).astype(jnp.bfloat16)
        return (
            attended,
            grad_query.astype(jnp.bfloat16),
            grad_key,
            grad_value,
            jnp.sum(grad_query, axis=0),
        )

    results = lax.map(one_head, jnp.arange(local_heads, dtype=jnp.int32))
    attended = merge_heads(results[0])
    grad_queries = merge_heads(results[1])
    grad_keys = merge_heads(results[2])
    grad_values = merge_heads(results[3])
    grad_bias = lax.psum(results[4], "ctx")
    outputs = (
        lax.all_to_all(attended, "tsp", split_axis=0, concat_axis=1, tiled=True),
        lax.all_to_all(grad_queries, "tsp", split_axis=0, concat_axis=1, tiled=True),
        lax.all_to_all(grad_keys, "tsp", split_axis=0, concat_axis=1, tiled=True),
        lax.all_to_all(grad_values, "tsp", split_axis=0, concat_axis=1, tiled=True),
    )
    return (outputs[0], outputs[1], outputs[2], outputs[3], grad_bias)


def solution(mesh):
    return jax.shard_map(
        shards,
        mesh=mesh,
        in_specs=(
            P(("ctx", "tsp"), None),
            P(("ctx", "tsp"), None),
            P(("ctx", "tsp"), None),
            P(("ctx", "tsp"), None),
            P("tsp", None),
            P("ctx"),
            P("ctx"),
        ),
        out_specs=(
            P(("ctx", "tsp"), None),
            P(("ctx", "tsp"), None),
            P(("ctx", "tsp"), None),
            P(("ctx", "tsp"), None),
            P("tsp", None),
        ),
        check_vma=False,
    )
```

profile of v0, /device:TPU:1, one launch (start us, length us, event | category | flops | bytes accessed | tf_op | source)
XLA Modules:
  0.0 595.5 jit_solution(16991121875115040467)
XLA Ops:
  3.2 4.8 all-to-all-start.1
  8.1 15.4 %all-to-all-done.1 = bf16[128,4,1280]{2,0,1:T(8,128)(2,1)} async-done(((bf16[128,4,1280]{2,0,1:T(8,128)(2,1)}), bf16[128,4,1280]{2,0,1:T(8,128)(2,1)}, u32[]{:S(2)}, u32[]{:S(2)}) %all-to-all-start.1) | async-done | bytes 1310752 | tf_op jit(solution)/shard_map/all_to_all | solution.py:28
  23.5 17.3 %all_to_all.152 = bf16[128,4,1280]{2,0,1:T(8,128)(2,1)} all-to-all(bf16[128,4,1280]{2,0,1:T(8,128)(2,1)S(1)} %bitcast.107), channel_id=1, replica_groups=mesh['ctx'=64,'tsp'=4] {'tsp'}, dimensions={1} | all-to-all | bytes 2621440 | tf_op jit(solution)/shard_map/all_to_all | solution.py:29
  42.8 10.0 %collective-permute-start = (bf16[2,512,1280]{2,1,0:T(8,128)(2,1)S(1)}, bf16[2,512,1280]{2,1,0:T(8,128)(2,1)S(1)}, u32[]{:S(2)}, u32[]{:S(2)}) collective-permute-start(bf16[2,512,1280]{2,1,0:T(8,128)(2,1)S(1)} %pad_maximum_fusion.7), channel_id=1, source_target_pairs={{0,4},{4,8},{8,12},{12,16},{16,20},{20,24},{24,28},{28,32},{32,36}... | collective-permute-start | bytes 7864328 | tf_op jit(solution)/shard_map/ppermute | solution.py:13
  52.9 28.6 %collective-permute-done = bf16[2,512,1280]{2,1,0:T(8,128)(2,1)S(1)} collective-permute-done((bf16[2,512,1280]{2,1,0:T(8,128)(2,1)S(1)}, bf16[2,512,1280]{2,1,0:T(8,128)(2,1)S(1)}, u32[]{:S(2)}, u32[]{:S(2)}) %collective-permute-start) | collective-permute-done | bytes 2621472 | tf_op jit(solution)/shard_map/ppermute | solution.py:13
  81.4 4.4 collective-permute-start.1
  85.8 28.6 %collective-permute-done.1 = bf16[2,512,1280]{2,1,0:T(8,128)(2,1)} collective-permute-done((bf16[2,512,1280]{2,1,0:T(8,128)(2,1)S(1)}, bf16[2,512,1280]{2,1,0:T(8,128)(2,1)}, u32[]{:S(2)}, u32[]{:S(2)}) %collective-permute-start.1) | collective-permute-done | bytes 2621472 | tf_op jit(solution)/shard_map/ppermute | solution.py:13
  114.4 4.5 collective-permute-start.2
  120.1 4.3 all-to-all-start
  128.3 14.5 %all-to-all-done = bf16[128,4,1280]{2,0,1:T(8,128)(2,1)} async-done(((bf16[128,4,1280]{2,0,1:T(8,128)(2,1)}), bf16[128,4,1280]{2,0,1:T(8,128)(2,1)}, u32[]{:S(2)}, u32[]{:S(2)}) %all-to-all-start) | async-done | bytes 1310752 | tf_op jit(solution)/shard_map/all_to_all | solution.py:27
  142.8 4.3 all-to-all-start.3
  147.8 6.2 %pad_maximum_fusion.6 = bf16[2,1536,1280]{2,1,0:T(8,128)(2,1)} fusion(bf16[2,512,1280]{2,1,0:T(8,128)(2,1)S(1)} %collective-permute-done, bf16[2,512,1280]{2,1,0:T(8,128)(2,1)} %collective-permute-done.1, bf16[2,512,1280]{2,1,0:T(8,128)(2,1)} %collective-permute-done.2), kind=kLoop, calls=%fused_computation.45 | loop fusion | flops 23592960 | bytes 15728640 | tf_op jit(solution)/shard_map/concatenate | solution.py:42
  154.0 10.8 %all-to-all-done.3 = bf16[128,4,1280]{2,0,1:T(8,128)(2,1)} async-done(((bf16[128,4,1280]{2,0,1:T(8,128)(2,1)}), bf16[128,4,1280]{2,0,1:T(8,128)(2,1)}, u32[]{:S(2)}, u32[]{:S(2)}) %all-to-all-start.3) | async-done | bytes 1310752 | tf_op jit(solution)/shard_map/all_to_all | solution.py:30
  164.8 226.8 %while.19 = (s32[]{:T(128)}, bf16[10,512,128]{2,1,0:T(8,128)(2,1)}, bf16[10,512,128]{2,1,0:T(8,128)(2,1)}, bf16[10,512,128]{2,1,0:T(8,128)(2,1)}, bf16[10,512,12...) while((s32[]{:T(128)}, bf16[10,512,128]{2,1,0:T(8,128)(2,1)}, ...), condition=%wide.region_5.6_spmd.clone, body=%wide.region_0.5_spmd.clone.sunk | while | flops 1235941760 | bytes 64526704 | solution.py:111
  166.0 3.6 fusion.51
  188.7 3.6 fusion.51
  211.4 3.6 fusion.51
  234.0 3.6 fusion.51
  256.7 3.6 fusion.51
  279.4 3.6 fusion.51
  302.0 3.6 fusion.51
  324.7 3.6 fusion.51
  347.4 3.6 fusion.51
  370.1 3.6 fusion.51
  403.7 11.3 %all-to-all-done.4 = bf16[4,128,1280]{1,2,0:T(8,128)(2,1)S(1)} async-done(((bf16[4,128,1280]{1,2,0:T(8,128)(2,1)}), bf16[4,128,1280]{1,2,0:T(8,128)(2,1)S(1)}, u32[]{:S(2)}, u32[]{:S(2)}) %all-to-all-start.4) | async-done | bytes 1310752 | tf_op jit(solution)/shard_map/all_to_all | solution.py:118
  420.9 3.6 all_to_all.136
  427.0 7.2 %all-to-all-done.5 = bf16[4,128,1280]{1,2,0:T(8,128)(2,1)S(1)} async-done(((bf16[4,128,1280]{1,2,0:T(8,128)(2,1)}), bf16[4,128,1280]{1,2,0:T(8,128)(2,1)S(1)}, u32[]{:S(2)}, u32[]{:S(2)}) %all-to-all-start.5) | async-done | bytes 1310752 | tf_op jit(solution)/shard_map/all_to_all | solution.py:119
  434.2 4.5 all-to-all-start.6
  441.2 3.6 all_to_all.140
  447.3 5.9 all-to-all-done.6
  453.2 4.3 all-to-all-start.7
  457.5 130.3 %psum.7 = f32[10,128]{1,0:T(8,128)} all-reduce(f32[10,128]{1,0:T(8,128)S(1)} %get-tuple-element.85), channel_id=1, replica_groups=mesh['ctx'=64,'tsp'=4] {'ctx'}, use_global_device_ids=true, to_apply=%region_6.7 | all-reduce | flops 1280 | bytes 10240 | tf_op jit(solution)/shard_map/psum | solution.py:116
  (197 shorter events, 207.3 us)
Async XLA Ops:
  0.6 7.4 %copy-start.1 = (bf16[128,5120]{1,0:T(8,128)(2,1)S(1)}, bf16[128,5120]{1,0:T(8,128)(2,1)}, u32[]{:S(2)}) copy-start(bf16[128,5120]{1,0:T(8,128)(2,1)} %param.11) | copy-start | bytes 3932164
  3.2 20.3 %all-to-all-start.1 = ((bf16[128,4,1280]{2,0,1:T(8,128)(2,1)}), bf16[128,4,1280]{2,0,1:T(8,128)(2,1)}, u32[]{:S(2)}, u32[]{:S(2)}) async-start(bf16[128,4,1280]{2,0,1:T(8,128)(2,1)} %bitcast.80), calls=%async_computation.1 | async-start | bytes 2621440 | tf_op jit(solution)/shard_map/all_to_all | solution.py:28
  40.8 78.1 %copy-start.2 = (bf16[128,5120]{1,0:T(8,128)(2,1)S(1)}, bf16[128,5120]{1,0:T(8,128)(2,1)}, u32[]{:S(2)}) copy-start(bf16[128,5120]{1,0:T(8,128)(2,1)} %param.9) | copy-start | bytes 3932164
  42.8 38.6 %collective-permute-start = (bf16[2,512,1280]{2,1,0:T(8,128)(2,1)S(1)}, bf16[2,512,1280]{2,1,0:T(8,128)(2,1)S(1)}, u32[]{:S(2)}, u32[]{:S(2)}) collective-permute-start(bf16[2,512,1280]{2,1,0:T(8,128)(2,1)S(1)} %pad_maximum_fusion.7), channel_id=1, source_target_pairs={{0,4},{4,8},{8,12},{12,16},{16,20},{20,24},{24,28},{28,32},{32,36}... | collective-permute-start | bytes 7864328 | tf_op jit(solution)/shard_map/ppermute | solution.py:13
  81.4 33.0 %collective-permute-start.1 = (bf16[2,512,1280]{2,1,0:T(8,128)(2,1)S(1)}, bf16[2,512,1280]{2,1,0:T(8,128)(2,1)}, u32[]{:S(2)}, u32[]{:S(2)}) collective-permute-start(bf16[2,512,1280]{2,1,0:T(8,128)(2,1)S(1)} %collective-permute-done), channel_id=1, source_target_pairs={{0,4},{4,8},{8,12},{12,16},{16,20},{20,24},{24,28},{28,32},{32,36}... | collective-permute-start | bytes 7864328 | tf_op jit(solution)/shard_map/ppermute | solution.py:13
  114.4 33.4 %collective-permute-start.2 = (bf16[2,512,1280]{2,1,0:T(8,128)(2,1)}, bf16[2,512,1280]{2,1,0:T(8,128)(2,1)}, u32[]{:S(2)}, u32[]{:S(2)}) collective-permute-start(bf16[2,512,1280]{2,1,0:T(8,128)(2,1)} %collective-permute-done.1), channel_id=1, source_target_pairs={{0,4},{4,8},{8,12},{12,16},{16,20},{20,24},{24,28},{28,32},{32,36}... | collective-permute-start | bytes 7864328 | tf_op jit(solution)/shard_map/ppermute | solution.py:13
  120.1 22.7 %all-to-all-start = ((bf16[128,4,1280]{2,0,1:T(8,128)(2,1)}), bf16[128,4,1280]{2,0,1:T(8,128)(2,1)}, u32[]{:S(2)}, u32[]{:S(2)}) async-start(bf16[128,4,1280]{2,0,1:T(8,128)(2,1)} %bitcast.81), calls=%async_computation | async-start | bytes 2621440 | tf_op jit(solution)/shard_map/all_to_all | solution.py:27
  142.8 22.0 %all-to-all-start.3 = ((bf16[128,4,1280]{2,0,1:T(8,128)(2,1)}), bf16[128,4,1280]{2,0,1:T(8,128)(2,1)}, u32[]{:S(2)}, u32[]{:S(2)}) async-start(bf16[128,4,1280]{2,0,1:T(8,128)(2,1)} %bitcast.78), calls=%async_computation.3 | async-start | bytes 2621440 | tf_op jit(solution)/shard_map/all_to_all | solution.py:30
  180.6 1.5 copy-start
  203.2 1.4 copy-start
  225.9 1.4 copy-start
  248.5 1.4 copy-start
  271.2 1.4 copy-start
  293.9 1.4 copy-start
  316.5 1.4 copy-start
  339.2 1.5 copy-start
  361.9 1.5 copy-start
  384.6 1.5 copy-start
  394.7 20.2 %all-to-all-start.4 = ((bf16[4,128,1280]{1,2,0:T(8,128)(2,1)}), bf16[4,128,1280]{1,2,0:T(8,128)(2,1)S(1)}, u32[]{:S(2)}, u32[]{:S(2)}) async-start(bf16[4,128,1280]{1,2,0:T(8,128)(2,1)} %copy.45), calls=%async_computation.4 | async-start | bytes 2621440 | tf_op jit(solution)/shard_map/all_to_all | solution.py:118
  414.9 19.3 %all-to-all-start.5 = ((bf16[4,128,1280]{1,2,0:T(8,128)(2,1)}), bf16[4,128,1280]{1,2,0:T(8,128)(2,1)S(1)}, u32[]{:S(2)}, u32[]{:S(2)}) async-start(bf16[4,128,1280]{1,2,0:T(8,128)(2,1)} %copy.47), calls=%async_computation.5 | async-start | bytes 2621440 | tf_op jit(solution)/shard_map/all_to_all | solution.py:119
  434.2 18.9 %all-to-all-start.6 = ((bf16[4,128,1280]{1,2,0:T(8,128)(2,1)}), bf16[4,128,1280]{1,2,0:T(8,128)(2,1)}, u32[]{:S(2)}, u32[]{:S(2)}) async-start(bf16[4,128,1280]{1,2,0:T(8,128)(2,1)} %copy.49), calls=%async_computation.6 | async-start | bytes 2621440 | tf_op jit(solution)/shard_map/all_to_all | solution.py:120
  453.2 139.9 %all-to-all-start.7 = ((bf16[4,128,1280]{1,2,0:T(8,128)(2,1)}), bf16[4,128,1280]{1,2,0:T(8,128)(2,1)}, u32[]{:S(2)}, u32[]{:S(2)}) async-start(bf16[4,128,1280]{1,2,0:T(8,128)(2,1)} %copy.51), calls=%async_computation.7 | async-start | bytes 2621440 | tf_op jit(solution)/shard_map/all_to_all | solution.py:121
where the time goes:
time: 598 us; the launch traced here: 595 us
  blocking collectives  148 us (25%)
  waiting for transfers between devices  123 us (21%)
  matrix products  118 us (20%)
  local copies, waits for them, and re-layouts  99.6 us (17%)
  starting transfers between devices  48.2 us (8%)
  other arithmetic  31.5 us (5%)
  loops' own time  25.9 us (4%)
    psum x1, blocking collectives, shards(): grad_bias = lax.psum(results[4], 'ctx')  130 us
    ppermute x3, waiting for transfers between devices, passed_along(): lax.ppermute(value, axis, [(source, source + steps) for source in range(i...  57.9 us
    slice x10, local copies, waits for them, and re-layouts, one_head(): window[1]  36 us
    dot_general x10, matrix products, one_head(): lax.dot_general(shifted, key_rows, contract_cols, preferred_element_type=...  29.1 us
    another operation x1, loops' own time, shards(): results = lax.map(one_head, jnp.arange(local_heads, dtype=jnp.int32))  25.9 us
    dot_general x10, matrix products, one_head(): lax.dot_general(grad_scores[:, MEM:], shifted, contract_rows, preferred_e...  20.8 us
    dot_general x10, matrix products, one_head(): lax.dot_general(grad_rows, value_rows, contract_cols, preferred_element_t...  20.7 us
    dot_general x10, matrix products, one_head(): lax.dot_general(probs_half[:, MEM:], grad_rows, contract_rows, preferred_...  19.1 us
  transfers between devices with their start and end apart: 10, of which 9 were waited for; matrix products, arithmetic and copies ran while one was open for 5% of the time, Pallas kernels for 0%

commit v1 on v0

--- a/solution.py
+++ b/solution.py
@@ -113,7 +113,9 @@
     grad_queries = merge_heads(results[1])
     grad_keys = merge_heads(results[2])
     grad_values = merge_heads(results[3])
-    grad_bias = lax.psum(results[4], "ctx")
+    part = results[4]
+    parts = lax.all_gather(part, "ctx")
+    grad_bias = jnp.sum(parts, axis=0)
     outputs = (
         lax.all_to_all(attended, "tsp", split_axis=0, concat_axis=1, tiled=True),
         lax.all_to_all(grad_queries, "tsp", split_axis=0, concat_axis=1, tiled=True),

time: 598 us -> 526 us (0.88)
  blocking collectives: 148 us -> 74.2 us
    psum x1 -> x0, blocking collectives: 130 us -> none  [shards(): grad_bias = lax.psum(results[4], 'ctx')]
    all_gather x0 -> x1, blocking collectives: none -> 56.9 us  [shards(): parts = lax.all_gather(part, 'ctx')]
  transfers between devices with their start and end apart: 10 -> 10, of which waited for: 9 -> 9; matrix products, arithmetic and copies ran while one was open for 5% -> 6% of each run, Pallas kernels for 0% -> 0%
where the time goes in v1:
time: 526 us; the launch traced here: 523 us
  waiting for transfers between devices  123 us (23%)
  matrix products  118 us (22%)
  local copies, waits for them, and re-layouts  99.6 us (19%)
  blocking collectives  74.2 us (14%)
  starting transfers between devices  48.2 us (9%)
  other arithmetic  32.2 us (6%)
  loops' own time  25.9 us (5%)
    ppermute x3, waiting for transfers between devices, passed_along(): lax.ppermute(value, axis, [(source, source + steps) for source in range(i...  57.9 us
    all_gather x1, blocking collectives, shards(): parts = lax.all_gather(part, 'ctx')  56.9 us
    slice x10, local copies, waits for them, and re-layouts, one_head(): window[1]  36 us
    dot_general x10, matrix products, one_head(): lax.dot_general(shifted, key_rows, contract_cols, preferred_element_type=...  29.1 us
    another operation x1, loops' own time, shards(): results = lax.map(one_head, jnp.arange(local_heads, dtype=jnp.int32))  25.9 us
    dot_general x10, matrix products, one_head(): lax.dot_general(grad_scores[:, MEM:], shifted, contract_rows, preferred_e...  20.8 us
    dot_general x10, matrix products, one_head(): lax.dot_general(grad_rows, value_rows, contract_cols, preferred_element_t...  20.8 us
    dot_general x10, matrix products, one_head(): lax.dot_general(probs_half[:, MEM:], grad_rows, contract_rows, preferred_...  19.1 us
  transfers between devices with their start and end apart: 10, of which 9 were waited for; matrix products, arithmetic and copies ran while one was open for 6% of the time, Pallas kernels for 0%

profile of v1, /device:TPU:1, one launch (start us, length us, event | category | flops | bytes accessed | tf_op | source)
XLA Modules:
  0.0 522.8 jit_solution(8765145533249923163)
XLA Ops:
  3.2 4.8 all-to-all-start.1
  8.1 15.4 %all-to-all-done.1 = bf16[128,4,1280]{2,0,1:T(8,128)(2,1)} async-done(((bf16[128,4,1280]{2,0,1:T(8,128)(2,1)}), bf16[128,4,1280]{2,0,1:T(8,128)(2,1)}, u32[]{:S(2)}, u32[]{:S(2)}) %all-to-all-start.1) | async-done | bytes 1310752 | tf_op jit(solution)/shard_map/all_to_all | solution.py:28
  23.5 17.3 %all_to_all.152 = bf16[128,4,1280]{2,0,1:T(8,128)(2,1)} all-to-all(bf16[128,4,1280]{2,0,1:T(8,128)(2,1)S(1)} %bitcast.108), channel_id=1, replica_groups=mesh['ctx'=64,'tsp'=4] {'tsp'}, dimensions={1} | all-to-all | bytes 2621440 | tf_op jit(solution)/shard_map/all_to_all | solution.py:29
  42.8 10.0 %collective-permute-start = (bf16[2,512,1280]{2,1,0:T(8,128)(2,1)S(1)}, bf16[2,512,1280]{2,1,0:T(8,128)(2,1)S(1)}, u32[]{:S(2)}, u32[]{:S(2)}) collective-permute-start(bf16[2,512,1280]{2,1,0:T(8,128)(2,1)S(1)} %pad_maximum_fusion.7), channel_id=1, source_target_pairs={{0,4},{4,8},{8,12},{12,16},{16,20},{20,24},{24,28},{28,32},{32,36}... | collective-permute-start | bytes 7864328 | tf_op jit(solution)/shard_map/ppermute | solution.py:13
  52.9 28.6 %collective-permute-done = bf16[2,512,1280]{2,1,0:T(8,128)(2,1)S(1)} collective-permute-done((bf16[2,512,1280]{2,1,0:T(8,128)(2,1)S(1)}, bf16[2,512,1280]{2,1,0:T(8,128)(2,1)S(1)}, u32[]{:S(2)}, u32[]{:S(2)}) %collective-permute-start) | collective-permute-done | bytes 2621472 | tf_op jit(solution)/shard_map/ppermute | solution.py:13
  81.4 4.4 collective-permute-start.1
  85.8 28.6 %collective-permute-done.1 = bf16[2,512,1280]{2,1,0:T(8,128)(2,1)} collective-permute-done((bf16[2,512,1280]{2,1,0:T(8,128)(2,1)S(1)}, bf16[2,512,1280]{2,1,0:T(8,128)(2,1)}, u32[]{:S(2)}, u32[]{:S(2)}) %collective-permute-start.1) | collective-permute-done | bytes 2621472 | tf_op jit(solution)/shard_map/ppermute | solution.py:13
  114.4 4.5 collective-permute-start.2
  120.1 4.3 all-to-all-start
  128.3 14.5 %all-to-all-done = bf16[128,4,1280]{2,0,1:T(8,128)(2,1)} async-done(((bf16[128,4,1280]{2,0,1:T(8,128)(2,1)}), bf16[128,4,1280]{2,0,1:T(8,128)(2,1)}, u32[]{:S(2)}, u32[]{:S(2)}) %all-to-all-start) | async-done | bytes 1310752 | tf_op jit(solution)/shard_map/all_to_all | solution.py:27
  142.8 4.3 all-to-all-start.3
  147.8 6.2 %pad_maximum_fusion.6 = bf16[2,1536,1280]{2,1,0:T(8,128)(2,1)} fusion(bf16[2,512,1280]{2,1,0:T(8,128)(2,1)S(1)} %collective-permute-done, bf16[2,512,1280]{2,1,0:T(8,128)(2,1)} %collective-permute-done.1, bf16[2,512,1280]{2,1,0:T(8,128)(2,1)} %collective-permute-done.2), kind=kLoop, calls=%fused_computation.45 | loop fusion | flops 23592960 | bytes 15728640 | tf_op jit(solution)/shard_map/concatenate | solution.py:42
  154.0 10.8 %all-to-all-done.3 = bf16[128,4,1280]{2,0,1:T(8,128)(2,1)} async-done(((bf16[128,4,1280]{2,0,1:T(8,128)(2,1)}), bf16[128,4,1280]{2,0,1:T(8,128)(2,1)}, u32[]{:S(2)}, u32[]{:S(2)}) %all-to-all-start.3) | async-done | bytes 1310752 | tf_op jit(solution)/shard_map/all_to_all | solution.py:30
  164.8 226.9 %while.19 = (s32[]{:T(128)}, bf16[10,512,128]{2,1,0:T(8,128)(2,1)}, bf16[10,512,128]{2,1,0:T(8,128)(2,1)}, bf16[10,512,128]{2,1,0:T(8,128)(2,1)}, bf16[10,512,12...) while((s32[]{:T(128)}, bf16[10,512,128]{2,1,0:T(8,128)(2,1)}, ...), condition=%wide.region_5.6_spmd.clone, body=%wide.region_0.5_spmd.clone.sunk | while | flops 1235941760 | bytes 64526704 | solution.py:111
  166.0 3.6 fusion.51
  188.7 3.6 fusion.51
  211.4 3.6 fusion.51
  234.1 3.6 fusion.51
  256.8 3.6 fusion.51
  279.4 3.6 fusion.51
  302.1 3.6 fusion.51
  324.8 3.6 fusion.51
  347.5 3.6 fusion.51
  370.2 3.6 fusion.51
  403.8 11.3 %all-to-all-done.4 = bf16[4,128,1280]{1,2,0:T(8,128)(2,1)S(1)} async-done(((bf16[4,128,1280]{1,2,0:T(8,128)(2,1)}), bf16[4,128,1280]{1,2,0:T(8,128)(2,1)S(1)}, u32[]{:S(2)}, u32[]{:S(2)}) %all-to-all-start.4) | async-done | bytes 1310752 | tf_op jit(solution)/shard_map/all_to_all | solution.py:120
  421.0 3.6 all_to_all.136
  427.1 7.2 %all-to-all-done.5 = bf16[4,128,1280]{1,2,0:T(8,128)(2,1)S(1)} async-done(((bf16[4,128,1280]{1,2,0:T(8,128)(2,1)}), bf16[4,128,1280]{1,2,0:T(8,128)(2,1)S(1)}, u32[]{:S(2)}, u32[]{:S(2)}) %all-to-all-start.5) | async-done | bytes 1310752 | tf_op jit(solution)/shard_map/all_to_all | solution.py:121
  434.3 4.5 all-to-all-start.6
  441.2 3.6 all_to_all.140
  447.3 5.9 %all-to-all-done.6 = bf16[4,128,1280]{1,2,0:T(8,128)(2,1)} async-done(((bf16[4,128,1280]{1,2,0:T(8,128)(2,1)}), bf16[4,128,1280]{1,2,0:T(8,128)(2,1)}, u32[]{:S(2)}, u32[]{:S(2)}) %all-to-all-start.6) | async-done | bytes 1310752 | tf_op jit(solution)/shard_map/all_to_all | solution.py:122
  453.2 4.3 all-to-all-start.7
  457.5 56.9 %all-gather.1 = f32[64,10,128]{2,1,0:T(8,128)S(1)} all-gather(f32[1,10,128]{2,1,0:T(8,128)S(1)} %bitcast.118), channel_id=2, replica_groups=mesh['ctx'=64,'tsp'=4] {'ctx'}, dimensions={0}, use_global_device_ids=true | all-gather | bytes 332800 | tf_op jit(solution)/shard_map/all_gather | solution.py:117
  (198 shorter events, 208.1 us)
Async XLA Ops:
  0.6 7.4 %copy-start.1 = (bf16[128,5120]{1,0:T(8,128)(2,1)S(1)}, bf16[128,5120]{1,0:T(8,128)(2,1)}, u32[]{:S(2)}) copy-start(bf16[128,5120]{1,0:T(8,128)(2,1)} %param.11) | copy-start | bytes 3932164
  3.2 20.3 %all-to-all-start.1 = ((bf16[128,4,1280]{2,0,1:T(8,128)(2,1)}), bf16[128,4,1280]{2,0,1:T(8,128)(2,1)}, u32[]{:S(2)}, u32[]{:S(2)}) async-start(bf16[128,4,1280]{2,0,1:T(8,128)(2,1)} %bitcast.81), calls=%async_computation.1 | async-start | bytes 2621440 | tf_op jit(solution)/shard_map/all_to_all | solution.py:28
  40.8 78.1 %copy-start.2 = (bf16[128,5120]{1,0:T(8,128)(2,1)S(1)}, bf16[128,5120]{1,0:T(8,128)(2,1)}, u32[]{:S(2)}) copy-start(bf16[128,5120]{1,0:T(8,128)(2,1)} %param.9) | copy-start | bytes 3932164
  42.8 38.6 %collective-permute-start = (bf16[2,512,1280]{2,1,0:T(8,128)(2,1)S(1)}, bf16[2,512,1280]{2,1,0:T(8,128)(2,1)S(1)}, u32[]{:S(2)}, u32[]{:S(2)}) collective-permute-start(bf16[2,512,1280]{2,1,0:T(8,128)(2,1)S(1)} %pad_maximum_fusion.7), channel_id=1, source_target_pairs={{0,4},{4,8},{8,12},{12,16},{16,20},{20,24},{24,28},{28,32},{32,36}... | collective-permute-start | bytes 7864328 | tf_op jit(solution)/shard_map/ppermute | solution.py:13
  81.4 33.0 %collective-permute-start.1 = (bf16[2,512,1280]{2,1,0:T(8,128)(2,1)S(1)}, bf16[2,512,1280]{2,1,0:T(8,128)(2,1)}, u32[]{:S(2)}, u32[]{:S(2)}) collective-permute-start(bf16[2,512,1280]{2,1,0:T(8,128)(2,1)S(1)} %collective-permute-done), channel_id=1, source_target_pairs={{0,4},{4,8},{8,12},{12,16},{16,20},{20,24},{24,28},{28,32},{32,36}... | collective-permute-start | bytes 7864328 | tf_op jit(solution)/shard_map/ppermute | solution.py:13
  114.4 33.4 %collective-permute-start.2 = (bf16[2,512,1280]{2,1,0:T(8,128)(2,1)}, bf16[2,512,1280]{2,1,0:T(8,128)(2,1)}, u32[]{:S(2)}, u32[]{:S(2)}) collective-permute-start(bf16[2,512,1280]{2,1,0:T(8,128)(2,1)} %collective-permute-done.1), channel_id=1, source_target_pairs={{0,4},{4,8},{8,12},{12,16},{16,20},{20,24},{24,28},{28,32},{32,36}... | collective-permute-start | bytes 7864328 | tf_op jit(solution)/shard_map/ppermute | solution.py:13
  120.1 22.7 %all-to-all-start = ((bf16[128,4,1280]{2,0,1:T(8,128)(2,1)}), bf16[128,4,1280]{2,0,1:T(8,128)(2,1)}, u32[]{:S(2)}, u32[]{:S(2)}) async-start(bf16[128,4,1280]{2,0,1:T(8,128)(2,1)} %bitcast.82), calls=%async_computation | async-start | bytes 2621440 | tf_op jit(solution)/shard_map/all_to_all | solution.py:27
  142.8 22.0 %all-to-all-start.3 = ((bf16[128,4,1280]{2,0,1:T(8,128)(2,1)}), bf16[128,4,1280]{2,0,1:T(8,128)(2,1)}, u32[]{:S(2)}, u32[]{:S(2)}) async-start(bf16[128,4,1280]{2,0,1:T(8,128)(2,1)} %bitcast.79), calls=%async_computation.3 | async-start | bytes 2621440 | tf_op jit(solution)/shard_map/all_to_all | solution.py:30
  180.5 1.5 copy-start
  203.2 1.4 copy-start
  225.9 1.4 copy-start
  248.6 1.4 copy-start
  271.3 1.4 copy-start
  293.9 1.4 copy-start
  316.6 1.4 copy-start
  339.3 1.5 copy-start
  362.0 1.5 copy-start
  384.7 1.5 copy-start
  394.8 20.2 %all-to-all-start.4 = ((bf16[4,128,1280]{1,2,0:T(8,128)(2,1)}), bf16[4,128,1280]{1,2,0:T(8,128)(2,1)S(1)}, u32[]{:S(2)}, u32[]{:S(2)}) async-start(bf16[4,128,1280]{1,2,0:T(8,128)(2,1)} %copy.45), calls=%async_computation.4 | async-start | bytes 2621440 | tf_op jit(solution)/shard_map/all_to_all | solution.py:120
  415.0 19.3 %all-to-all-start.5 = ((bf16[4,128,1280]{1,2,0:T(8,128)(2,1)}), bf16[4,128,1280]{1,2,0:T(8,128)(2,1)S(1)}, u32[]{:S(2)}, u32[]{:S(2)}) async-start(bf16[4,128,1280]{1,2,0:T(8,128)(2,1)} %copy.47), calls=%async_computation.5 | async-start | bytes 2621440 | tf_op jit(solution)/shard_map/all_to_all | solution.py:121
  434.3 18.9 %all-to-all-start.6 = ((bf16[4,128,1280]{1,2,0:T(8,128)(2,1)}), bf16[4,128,1280]{1,2,0:T(8,128)(2,1)}, u32[]{:S(2)}, u32[]{:S(2)}) async-start(bf16[4,128,1280]{1,2,0:T(8,128)(2,1)} %copy.49), calls=%async_computation.6 | async-start | bytes 2621440 | tf_op jit(solution)/shard_map/all_to_all | solution.py:122
  453.2 67.2 %all-to-all-start.7 = ((bf16[4,128,1280]{1,2,0:T(8,128)(2,1)}), bf16[4,128,1280]{1,2,0:T(8,128)(2,1)}, u32[]{:S(2)}, u32[]{:S(2)}) async-start(bf16[4,128,1280]{1,2,0:T(8,128)(2,1)} %copy.51), calls=%async_computation.7 | async-start | bytes 2621440 | tf_op jit(solution)/shard_map/all_to_all | solution.py:123
